TPU v7x, 32 devices: a whole 2x2x4 slice. The times are simulated.
32 devices in a mesh: shell: 4 (over x, core), tile: 8 (over z, y).
Axes of the slice: x: 2, y: 2, z: 4, core: 2. Of those that a mesh axis runs over, the one named last changes fastest.
Arguments:
- residual: bfloat16 [16, 131072], P('shell', 'tile'), may hold values from -6 to 6
- tile_ray: int32 [1024], P('tile'), may hold values from 0 to 127, as said below
- filter_rows: bfloat16 [128, 128], replicated, may hold values from -0.5 to 0.5
- filter_cols: bfloat16 [128, 128], replicated, may hold values from -0.5 to 0.5
- band_lo: int32 [16], replicated, may hold values from 0 to 8
- shell_weight: float32 [16], replicated, may hold values from 0.3 to 3
Outputs:
- shell_grad: bfloat16 [16, 131072], P('shell', 'tile')
Inputs may be any that keep to these rules, and one draw needn't show every extreme that they name: `tile_ray`: for each tile t, entries t * 128 to (t + 1) * 128 - 1 are a permutation of 0 to 127.
All inputs are finite; a program needn't handle non-finite values.
Results may differ from a plain program's by a relative error of at most 0.006.
Values may be sent and summed in bfloat16 or wider, within the bound.
A program may use at most 64 MiB of HBM per device.

v0:
```python
import jax
import jax.numpy as jnp
from jax import lax
from jax.sharding import PartitionSpec as P


def kernel_table(band_lo, shell_weight):
    count = shell_weight.shape[0]
    band = count // 2
    index = jnp.arange(count)
    chi_shell = (index.astype(jnp.float32) + 0.5) / count
    chi_source = (band_lo.astype(jnp.float32) + band) / count
    inside = (index[None, :] >= band_lo[:, None]) & (index[None, :] < band_lo[:, None] + band)
    values = (
        8.0
        * shell_weight[None, :]
        * chi_shell[None, :]
        * (chi_source[:, None] - chi_shell[None, :])
        / chi_source[:, None]
    )
    return jnp.where(inside, values, jnp.zeros_like(values)).astype(jnp.bfloat16)


def shards(residual, tile_ray, filter_rows, filter_cols, band_lo, shell_weight):
    planes, rays = residual.shape
    ntile = lax.axis_size("tile")
    run = rays // ntile
    side = filter_rows.shape[0]
    grouped = residual.reshape(planes, ntile, run)
    arrived = lax.all_to_all(grouped, "tile", split_axis=1, concat_axis=1, tiled=True).reshape(
        planes, side, side
    )
    image = jnp.take(arrived, tile_ray, axis=1)
    half = jnp.einsum("sik,kb->sib", image, filter_cols, preferred_element_type=jnp.float32)
    whole = lax.dot_general(
        half,
        filter_rows.astype(jnp.float32),
        (((1,), (0,)), ((), ())),
        precision=lax.Precision.HIGHEST,
    )
    smoothed = jnp.swapaxes(whole, 1, 2).astype(jnp.bfloat16).reshape(planes, rays)
    kernel = kernel_table(band_lo, shell_weight)
    mine = lax.axis_index("shell")
    own_cols = lax.dynamic_slice_in_dim(kernel, mine * planes, planes, 1)
    shell_grad = jnp.dot(
        own_cols.T,
        lax.all_gather(smoothed, "shell", axis=0, tiled=True),
        preferred_element_type=jnp.float32,
    )
    return shell_grad.astype(jnp.bfloat16)


def solution(mesh):
    in_specs = (P("shell", "tile"), P("tile"), P(), P(), P(), P())
    out_specs = P("shell", "tile")
    return jax.shard_map(shards, mesh=mesh, in_specs=in_specs, out_specs=out_specs, check_vma=False)
```

profile of v0, /device:TPU:0, one launch (start us, length us, event | category | flops | bytes accessed | tf_op | source)
XLA Modules:
  0.0 25.3 jit_solution(11491204876930860951)
XLA Ops:
  0.0 0.0 copy-start
  0.0 0.0 copy-start.3
  0.0 7.4 %all-to-all-start = ((bf16[4,8,2048]{2,0,1:T(4,128)(2,1)}), bf16[4,8,2048]{2,0,1:T(4,128)(2,1)S(1)}, u32[]{:S(2)}, u32[]{:S(2)}) async-start(bf16[4,8,2048]{2,0,1:T(4,128)(2,1)} %bitcast.15), calls=%async_computation | async-start | bytes 262144 | tf_op jit(solution)/shard_map/all_to_all | solution.py:30
  7.4 0.0 copy-done.3
  7.4 0.0 copy-start.4
  7.5 0.6 %copy-done.4 = f32[16]{0:T(128)S(1)} copy-done((f32[16]{0:T(128)S(1)}, f32[16]{0:T(128)}, u32[]{:S(2)}) %copy-start.4) | copy-done | bytes 88
  8.1 0.0 copy-start.2
  8.1 0.6 %copy-done.2 = s32[16]{0:T(128)S(1)} copy-done((s32[16]{0:T(128)S(1)}, s32[16]{0:T(128)}, u32[]{:S(2)}) %copy-start.2) | copy-done | bytes 88
  8.8 0.1 dynamic-slice.1
  8.8 0.1 dynamic-slice
  8.9 5.8 %all-to-all-done = bf16[4,8,2048]{2,0,1:T(4,128)(2,1)S(1)} async-done(((bf16[4,8,2048]{2,0,1:T(4,128)(2,1)}), bf16[4,8,2048]{2,0,1:T(4,128)(2,1)S(1)}, u32[]{:S(2)}, u32[]{:S(2)}) %all-to-all-start) | async-done | bytes 131104 | tf_op jit(solution)/shard_map/all_to_all | solution.py:30
  14.8 0.7 %gather_fusion = bf16[128,4,128]{2,1,0:T(4,128)(2,1)S(1)} fusion(bf16[4,128,128]{2,0,1:T(4,128)(2,1)S(1)} %bitcast.14, s32[1024]{0:T(1024)S(1)} %pad_clamp_fusion), kind=kCustom, calls=%fused_computation | custom fusion | bytes 262656 | tf_op jit(solution)/shard_map/jit(_take)/gather | solution.py:33
  15.5 0.2 select_bitcast_fusion
  15.7 0.0 copy-done
  15.7 0.0 copy-start.1
  15.7 0.2 fusion.1
  16.0 0.5 %copy-done.1 = bf16[128,128]{1,0:T(8,128)(2,1)S(1)} copy-done((bf16[128,128]{1,0:T(8,128)(2,1)S(1)}, bf16[128,128]{1,0:T(8,128)(2,1)}, u32[]{:S(2)}) %copy-start.1) | copy-done | bytes 32792
  16.5 0.3 %fusion = bf16[4,128,128]{1,2,0:T(8,128)(2,1)S(1)} fusion(f32[4,128,128]{1,2,0:T(8,128)S(1)} %fusion.1, bf16[128,128]{1,0:T(8,128)(2,1)S(1)} %copy-done.1), kind=kOutput, calls=%fused_computation.3 | convolution fusion | flops 100728832 | bytes 425984 | tf_op jit(solution)/shard_map/dot_general | solution.py:35
  16.8 0.1 copy.16
  17.0 7.2 %all-gather = bf16[4,4,16384]{2,1,0:T(4,128)(2,1)S(1)} all-gather(bf16[1,4,16384]{2,1,0:T(4,128)(2,1)S(1)} %reshape.39), channel_id=1, replica_groups=mesh['shell'=4,'tile'=8] {'shell'}, dimensions={0}, use_global_device_ids=true | all-gather | bytes 655360 | tf_op jit(solution)/shard_map/all_gather | solution.py:47
  24.1 0.1 reshape.40
  24.3 1.0 %convolution_convert_fusion = bf16[4,16384]{1,0:T(4,128)(2,1)} fusion(bf16[16,16384]{1,0:T(8,128)(2,1)S(1)} %reshape.40, f32[4]{0:T(128)S(1)} %dynamic-slice.1, s32[16]{0:T(128)S(1)} %broadcast_add_fusion, s32[16]{0:T(128)S(1)} %copy-done.2, s32[]{:T(128)S(6)} %select_n.17, f32[4]{0:T(128)S(1)} %dynamic-slice, f32[16]{0:T(128)S(1)} %add_multiply_fusion), kind=kOutput, calls=%fused_computation.1 | convolution fusion | flops 2163264 | bytes 655588 | tf_op jit(solution)/shard_map/dot_general | solution.py:45
  (8 shorter events, 0.1 us)
Async XLA Ops:
  0.0 15.7 %copy-start = (bf16[128,128]{1,0:T(8,128)(2,1)S(1)}, bf16[128,128]{1,0:T(8,128)(2,1)}, u32[]{:S(2)}) copy-start(bf16[128,128]{1,0:T(8,128)(2,1)} %param.9) | copy-start | bytes 98308
  0.0 7.4 %copy-start.3 = (s32[128]{0:T(128)S(1)}, s32[128]{0:T(128)}, u32[]{:S(2)}) copy-start(s32[128]{0:T(128)} %param.7) | copy-start | bytes 1540
  0.0 14.8 %all-to-all-start = ((bf16[4,8,2048]{2,0,1:T(4,128)(2,1)}), bf16[4,8,2048]{2,0,1:T(4,128)(2,1)S(1)}, u32[]{:S(2)}, u32[]{:S(2)}) async-start(bf16[4,8,2048]{2,0,1:T(4,128)(2,1)} %bitcast.15), calls=%async_computation | async-start | bytes 262144 | tf_op jit(solution)/shard_map/all_to_all | solution.py:30
  7.4 0.7 %copy-start.4 = (f32[16]{0:T(128)S(1)}, f32[16]{0:T(128)}, u32[]{:S(2)}) copy-start(f32[16]{0:T(128)} %param.11) | copy-start | bytes 196
  8.1 0.7 %copy-start.2 = (s32[16]{0:T(128)S(1)}, s32[16]{0:T(128)}, u32[]{:S(2)}) copy-start(s32[16]{0:T(128)} %param.10) | copy-start | bytes 196
  15.7 0.8 %copy-start.1 = (bf16[128,128]{1,0:T(8,128)(2,1)S(1)}, bf16[128,128]{1,0:T(8,128)(2,1)}, u32[]{:S(2)}) copy-start(bf16[128,128]{1,0:T(8,128)(2,1)} %param.8) | copy-start | bytes 98308
where the time goes:
time: 25.6 us; the launch traced here: 25.3 us
  starting transfers between devices  7.41 us (29%)
  blocking collectives  7.17 us (28%)
  waiting for transfers between devices  5.84 us (23%)
  local copies, waits for them, and re-layouts  3.01 us (12%)
  matrix products  1.49 us (6%)
    all_to_all x1, starting transfers between devices, shards(): lax.all_to_all(grouped, 'tile', split_axis=1, concat_axis=1, tiled=True)  7.41 us
    all_gather x1, blocking collectives, shards(): lax.all_gather(smoothed, 'shell', axis=0, tiled=True)  7.17 us
    all_to_all x1, waiting for transfers between devices, shards(): lax.all_to_all(grouped, 'tile', split_axis=1, concat_axis=1, tiled=True)  5.84 us
    unnamed x12, local copies, waits for them, and re-layouts  1.99 us
    dot_general x1, matrix products, shards(): jnp.dot(own_cols.T, lax.all_gather(smoothed, 'shell', axis=0, tiled=True)...  1.01 us
    gather x1, local copies, waits for them, and re-layouts, shards(): image = jnp.take(arrived, tile_ray, axis=1)  0.74 us
  transfers between devices with their start and end apart: 1, of which 1 were waited for; matrix products, arithmetic and copies ran while one was open for 1% of the time, Pallas kernels for 0%

commit v1 on v0

v1 whole, which is shorter than its diff:
```python
import functools

import jax
import jax.numpy as jnp
from jax import lax
from jax.experimental import pallas as pl
from jax.experimental.pallas import tpu as pltpu
from jax.sharding import PartitionSpec as P

MESH = pl.DeviceIdType.MESH
CORES = 2
F32 = jnp.float32
BF16 = jnp.bfloat16


def body(
    nshell, ntile, planes, group,
    rays, order, rows_in, cols_in, low_in, weight_in,
    out,
    recv, gath, half, acc, order_v, rows_v, cols_v, low_s, weight_s, table,
    local_sem, own_sem, a2a_send, a2a_recv, x_send, near_send, fwd_send, shell_recv,
):
    side = rows_v.shape[0]
    count = nshell * planes
    band = count // 2
    blk = rays.shape[0] // ntile
    nx = nshell // CORES
    sh, ti = lax.axis_index("shell"), lax.axis_index("tile")
    xi, core = sh // CORES, lax.rem(sh, CORES)
    partner = xi * CORES + (1 - core)

    def xpeer(e):
        return lax.rem(xi + e, nx) * CORES + core

    loads = [
        pltpu.make_async_copy(src, dst, local_sem.at[i])
        for i, (src, dst) in enumerate(
            [(order, order_v), (rows_in, rows_v), (cols_in, cols_v), (low_in, low_s), (weight_in, weight_s)]
        )
    ]

    barrier = pltpu.get_barrier_semaphore()

    def greet(e, _):
        pl.semaphore_signal(barrier, inc=1, device_id=(sh, lax.rem(ti + e, ntile)), device_id_type=MESH)
        return 0

    lax.fori_loop(1, ntile, greet, 0)
    pl.semaphore_signal(barrier, inc=1, device_id=(partner, ti), device_id_type=MESH)
    for e in range(1, nx):
        pl.semaphore_signal(barrier, inc=1, device_id=(xpeer(e), ti), device_id_type=MESH)

    for load in loads:
        load.start()
    own = pltpu.make_async_copy(rays.at[pl.ds(ti * blk, blk)], recv.at[pl.ds(ti * blk, blk)], own_sem)
    own.start()
    pl.semaphore_wait(barrier, ntile - 1 + nx)

    def block_to(e):
        to = lax.rem(ti + e, ntile)
        return pltpu.make_async_remote_copy(
            src_ref=rays.at[pl.ds(to * blk, blk)],
            dst_ref=recv.at[pl.ds(ti * blk, blk)],
            send_sem=a2a_send.at[e - 1],
            recv_sem=a2a_recv.at[e - 1],
            device_id=(sh, to),
            device_id_type=MESH,
        )

    def send(e, _):
        block_to(e).start()
        return 0

    lax.fori_loop(1, ntile, send, 0)

    for load in loads:
        load.wait()
    spot = lax.broadcasted_iota(jnp.int32, (side, side), 0)
    onehot = jnp.where(spot == order_v[...], 1.0, 0.0).astype(BF16)
    permuted = jnp.dot(onehot, rows_v[...], preferred_element_type=F32)
    filt = permuted.T.astype(BF16)
    cols = cols_v[...]

    which = lax.broadcasted_iota(jnp.int32, (count, side), 0)
    low = jnp.zeros((count, side), jnp.int32)
    for s in range(count):
        low = jnp.where(which == s, low_s[s], low)
    chi_source = (low.astype(F32) + band) / count
    for j in range(planes):
        shell = sh * planes + j
        chi_shell = (jnp.zeros((count, side), jnp.int32) + shell).astype(F32)
        chi_shell = (chi_shell + 0.5) / count
        value = 8.0 * weight_s[shell] * chi_shell * (chi_source - chi_shell) / chi_source
        value = jnp.where((low <= shell) & (shell < low + band), value, 0.0)
        table[j] = value.astype(BF16).astype(F32)

    step = blk * group
    own.wait()

    def column(e, _):
        @pl.when(e > 0)
        def _():
            block_to(jnp.maximum(e, 1)).wait_recv()

        source = lax.rem(ti - e + ntile, ntile)
        part = recv[pl.ds(source * blk, blk)]
        part = part.astype(F32).reshape(step, side).astype(BF16)
        half[pl.ds(pl.multiple_of(source * step, step), step), :] = jnp.dot(part, cols, preferred_element_type=F32)
        return 0

    lax.fori_loop(0, ntile, column, 0)

    def shell_copy(s, source, target, send_sem):
        return pltpu.make_async_remote_copy(
            src_ref=gath.at[source, s],
            dst_ref=gath.at[source, s],
            send_sem=send_sem,
            recv_sem=shell_recv.at[source, s],
            device_id=(target, ti),
            device_id_type=MESH,
        )

    for s in range(planes):
        plane = half[pl.ds(s, side, stride=planes), :].astype(BF16)
        gath[sh, s] = jnp.dot(filt, plane, preferred_element_type=F32).astype(BF16)
        for e in range(1, nx):
            shell_copy(s, sh, xpeer(e), x_send.at[e - 1, s]).start()
        shell_copy(s, sh, partner, near_send.at[s]).start()

    chunk = side // 4

    def mix(source, first):
        for c in range(0, side, chunk):
            got = [gath[source, s, pl.ds(c, chunk), :].astype(F32) for s in range(planes)]
            for j in range(planes):
                place = pl.ds(c * planes + j, chunk, stride=planes)
                total = None if first else acc[place, :]
                for s in range(planes):
                    term = table[j, pl.ds(source * planes + s, 1), :] * got[s]
                    total = term if total is None else total + term
                acc[place, :] = total

    mix(sh, True)
    for s in range(planes):
        shell_copy(s, partner, sh, near_send.at[s]).wait_recv()
    mix(partner, False)
    for e in range(1, nx):
        source = xpeer(nx - e)
        for s in range(planes):
            shell_copy(s, source, sh, x_send.at[e - 1, s]).wait_recv()
            shell_copy(s, source, partner, fwd_send.at[e - 1, s]).start()
        mix(source, False)
    for e in range(1, nx):
        source = lax.rem(xi + nx - e, nx) * CORES + (1 - core)
        for s in range(planes):
            shell_copy(s, source, sh, fwd_send.at[e - 1, s]).wait_recv()
        mix(source, False)
    out[...] = acc[...].astype(BF16).reshape(out.shape)

    def sent(e, _):
        block_to(e).wait_send()
        return 0

    lax.fori_loop(1, ntile, sent, 0)
    for s in range(planes):
        shell_copy(s, sh, partner, near_send.at[s]).wait_send()
        for e in range(1, nx):
            shell_copy(s, sh, xpeer(e), x_send.at[e - 1, s]).wait_send()
            shell_copy(s, xpeer(nx - e), partner, fwd_send.at[e - 1, s]).wait_send()


def shards(residual, tile_ray, filter_rows, filter_cols, band_lo, shell_weight):
    planes, rays = residual.shape
    nshell, ntile = lax.axis_size("shell"), lax.axis_size("tile")
    side = filter_rows.shape[0]
    count = band_lo.shape[0]
    nx = nshell // CORES
    per = side // ntile
    fold = 4 if per % 4 == 0 else 1
    group = planes * fold
    major = side // fold
    arranged = residual.reshape(planes, side, side).transpose(1, 0, 2).reshape(major, group, side)
    dma = pltpu.SemaphoreType.DMA
    result = pl.pallas_call(
        functools.partial(body, nshell, ntile, planes, group),
        out_shape=jax.ShapeDtypeStruct((major, group, side), BF16),
        in_specs=[pl.BlockSpec(memory_space=pl.ANY)] * 6,
        out_specs=pl.BlockSpec(memory_space=pltpu.VMEM),
        scratch_shapes=[
            pltpu.VMEM((major, group, side), BF16),
            pltpu.VMEM((nshell, planes, side, side), BF16),
            pltpu.VMEM((side * planes, side), F32),
            pltpu.VMEM((side * planes, side), F32),
            pltpu.VMEM((1, side), jnp.int32),
            pltpu.VMEM((side, side), BF16),
            pltpu.VMEM((side, side), BF16),
            pltpu.SMEM((count,), jnp.int32),
            pltpu.SMEM((count,), F32),
            pltpu.VMEM((planes, count, side), F32),
            dma((5,)),
            dma,
            dma((ntile - 1,)),
            dma((ntile - 1,)),
            dma((nx - 1, planes)),
            dma((planes,)),
            dma((nx - 1, planes)),
            dma((nshell, planes)),
        ],
        compiler_params=pltpu.CompilerParams(
            collective_id=0, has_side_effects=True, vmem_limit_bytes=32 * 1024 * 1024
        ),
    )(arranged, tile_ray.reshape(1, side), filter_rows, filter_cols, band_lo, shell_weight)
    return result.reshape(side, planes, side).transpose(1, 0, 2).reshape(planes, rays)


def solution(mesh):
    in_specs = (P("shell", "tile"), P("tile"), P(), P(), P(), P())
    out_specs = P("shell", "tile")
    return jax.shard_map(shards, mesh=mesh, in_specs=in_specs, out_specs=out_specs, check_vma=False)
```

time: 25.6 us -> 19.9 us (0.78)
  Pallas kernels: 0 us -> 15.8 us
  starting transfers between devices: 7.41 us -> 0 us
  blocking collectives: 7.17 us -> 0 us
  waiting for transfers between devices: 5.84 us -> 0 us
  matrix products: 1.49 us -> 0 us
  local copies, waits for them, and re-layouts: 3.01 us -> 3.76 us
    pallas_call x0 -> x1, Pallas kernels: none -> 15.8 us  [shards(): pl.pallas_call(functools.partial(body, nshell, ntile, planes, group), out...]
    all_to_all x1 -> x0, starting transfers between devices: 7.41 us -> none  [shards(): lax.all_to_all(grouped, 'tile', split_axis=1, concat_axis=1, tiled=True)]
    all_gather x1 -> x0, blocking collectives: 7.17 us -> none  [shards(): lax.all_gather(smoothed, 'shell', axis=0, tiled=True)]
    all_to_all x1 -> x0, waiting for transfers between devices: 5.84 us -> none  [shards(): lax.all_to_all(grouped, 'tile', split_axis=1, concat_axis=1, tiled=True)]
    unnamed x12 -> x13, local copies, waits for them, and re-layouts: 1.99 us -> 3.76 us
    dot_general x3 -> x0, matrix products: 1.49 us -> none  [the longest x1 1.01 us: shards(): jnp.dot(own_cols.T, lax.all_gather(smoothed, 'shell', axis=0, tiled=True)...]
    gather x1 -> x0, local copies, waits for them, and re-layouts: 0.74 us -> none  [shards(): image = jnp.take(arrived, tile_ray, axis=1)]
  transfers between devices with their start and end apart: 1 -> 0, of which waited for: 1 -> 0; matrix products, arithmetic and copies ran while one was open for 1% -> 0% of each run, Pallas kernels for 0% -> 0%
where the time goes in v1:
time: 19.9 us; the launch traced here: 19.5 us
  Pallas kernels  15.8 us (79%)
  local copies, waits for them, and re-layouts  3.76 us (19%)
    pallas_call x1, Pallas kernels, shards(): pl.pallas_call(functools.partial(body, nshell, ntile, planes, group), out...  15.8 us
    unnamed x13, local copies, waits for them, and re-layouts  3.76 us

profile of v1, /device:TPU:0, one launch (start us, length us, event | category | flops | bytes accessed | tf_op | source)
XLA Modules:
  0.0 19.5 jit_solution(13006221584167786573)
XLA Ops:
  0.0 0.0 copy-start.3
  0.0 0.0 copy-start.4
  0.0 0.0 copy-start.5
  0.0 0.6 %copy-done.3 = s32[128]{0:T(128)S(1)} copy-done((s32[128]{0:T(128)S(1)}, s32[128]{0:T(128)}, u32[]{:S(2)}) %copy-start.3) | copy-done | bytes 536
  0.7 0.0 copy-done.4
  0.7 0.0 copy-done.5
  0.7 0.0 copy-start
  0.7 0.9 %copy-done = bf16[4,16384]{1,0:T(4,128)(2,1)S(1)} copy-done((bf16[4,16384]{1,0:T(4,128)(2,1)S(1)}, bf16[4,16384]{1,0:T(4,128)(2,1)}, u32[]{:S(2)}) %copy-start) | copy-done | bytes 131096
  1.6 0.0 copy-start.1
  1.6 0.8 %copy-done.1 = bf16[128,128]{1,0:T(8,128)(2,1)S(1)} copy-done((bf16[128,128]{1,0:T(8,128)(2,1)S(1)}, bf16[128,128]{1,0:T(8,128)(2,1)}, u32[]{:S(2)}) %copy-start.1) | copy-done | bytes 32792
  2.4 0.0 copy-start.2
  2.4 0.8 %copy-done.2 = bf16[128,128]{1,0:T(8,128)(2,1)S(1)} copy-done((bf16[128,128]{1,0:T(8,128)(2,1)S(1)}, bf16[128,128]{1,0:T(8,128)(2,1)}, u32[]{:S(2)}) %copy-start.2) | copy-done | bytes 32792
  3.1 15.8 %shard_map.64 = bf16[32,16,128]{2,1,0:T(8,128)(2,1)S(1)} custom-call(bf16[32,16,128]{2,1,0:T(8,128)(2,1)S(1)} %bitcast.12, s32[1,128]{1,0:T(1,128)S(1)} %bitcast.13, bf16[128,128]{1,0:T(8,128)(2,1)S(1)} %copy-done.1, bf16[128,128]{1,0:T(8,128)(2,1)S(1)} %copy-done.2, s32[16]{0:T(128)S(1)} %copy-done.4, f32[16]{0:T(128)S(1)} %copy-done.5), custom_call_target="tpu_custom_call" | custom-call | tf_op jit(solution)/shard_map/pallas_call | solution.py:184
  18.9 0.7 %copy.10 = bf16[4,16384]{1,0:T(4,128)(2,1)} copy(bf16[4,16384]{1,0:T(4,128)(2,1)S(1)} %bitcast.11) | data formatting | bytes 262144
Async XLA Ops:
  0.0 0.7 %copy-start.3 = (s32[128]{0:T(128)S(1)}, s32[128]{0:T(128)}, u32[]{:S(2)}) copy-start(s32[128]{0:T(128)} %param.7) | copy-start | bytes 1540
  0.0 0.7 %copy-start.4 = (s32[16]{0:T(128)S(1)}, s32[16]{0:T(128)}, u32[]{:S(2)}) copy-start(s32[16]{0:T(128)} %low_in.1) | copy-start | bytes 196
  0.0 0.7 %copy-start.5 = (f32[16]{0:T(128)S(1)}, f32[16]{0:T(128)}, u32[]{:S(2)}) copy-start(f32[16]{0:T(128)} %weight_in.1) | copy-start | bytes 196
  0.7 0.9 %copy-start = (bf16[4,16384]{1,0:T(4,128)(2,1)S(1)}, bf16[4,16384]{1,0:T(4,128)(2,1)}, u32[]{:S(2)}) copy-start(bf16[4,16384]{1,0:T(4,128)(2,1)} %param.6) | copy-start | bytes 393220
  1.6 0.8 %copy-start.1 = (bf16[128,128]{1,0:T(8,128)(2,1)S(1)}, bf16[128,128]{1,0:T(8,128)(2,1)}, u32[]{:S(2)}) copy-start(bf16[128,128]{1,0:T(8,128)(2,1)} %rows_in.1) | copy-start | bytes 98308
  2.4 0.8 %copy-start.2 = (bf16[128,128]{1,0:T(8,128)(2,1)S(1)}, bf16[128,128]{1,0:T(8,128)(2,1)}, u32[]{:S(2)}) copy-start(bf16[128,128]{1,0:T(8,128)(2,1)} %cols_in.1) | copy-start | bytes 98308

commit v2 on v1

v2 whole, which is shorter than its diff:
```python
import functools

import jax
import jax.numpy as jnp
from jax import lax
from jax.experimental import pallas as pl
from jax.experimental.pallas import tpu as pltpu
from jax.sharding import PartitionSpec as P

MESH = pl.DeviceIdType.MESH
CORES = 2
F32 = jnp.float32
BF16 = jnp.bfloat16


def body(
    nshell, ntile, planes,
    rays, order, rows_in, cols_in, low_in, weight_in,
    out,
    stage, leave, recv, gath, half, acc, order_v, rows_v, cols_v, low_s, weight_s, table,
    local_sem, a2a_send, a2a_recv, x_send, near_send, fwd_send, shell_recv,
):
    side = rows_v.shape[0]
    count = nshell * planes
    band = count // 2
    blk = side // ntile
    nx = nshell // CORES
    sh, ti = lax.axis_index("shell"), lax.axis_index("tile")
    xi, core = sh // CORES, lax.rem(sh, CORES)
    partner = xi * CORES + (1 - core)

    def xpeer(e):
        return lax.rem(xi + e, nx) * CORES + core

    barrier = pltpu.get_barrier_semaphore()

    def greet(e, _):
        pl.semaphore_signal(barrier, inc=1, device_id=(sh, lax.rem(ti + e, ntile)), device_id_type=MESH)
        return 0

    lax.fori_loop(1, ntile, greet, 0, unroll=ntile <= 8)
    pl.semaphore_signal(barrier, inc=1, device_id=(partner, ti), device_id_type=MESH)
    for e in range(1, nx):
        pl.semaphore_signal(barrier, inc=1, device_id=(xpeer(e), ti), device_id_type=MESH)

    pairs = [
        (rays, stage), (cols_in, cols_v), (order, order_v), (rows_in, rows_v), (low_in, low_s), (weight_in, weight_s)
    ]
    loads = [pltpu.make_async_copy(src, dst, local_sem.at[i]) for i, (src, dst) in enumerate(pairs)]
    for load in loads:
        load.start()

    loads[0].wait()
    loads[1].wait()
    mine = stage[...]
    if mine.shape[1] % 16:
        mine = mine.astype(F32).reshape(half.shape).astype(BF16)
    half[...] = jnp.dot(mine.reshape(half.shape), cols_v[...], preferred_element_type=F32)
    for s in range(planes):
        leave[s] = half[pl.ds(s, side, stride=planes), :].reshape(ntile, blk, side).astype(BF16)

    pl.semaphore_wait(barrier, ntile - 1 + nx)

    for s in range(planes):

        def send(e, _):
            to = lax.rem(ti + e, ntile)
            pltpu.make_async_remote_copy(
                src_ref=leave.at[s, to],
                dst_ref=recv.at[s, ti],
                send_sem=a2a_send,
                recv_sem=a2a_recv.at[s],
                device_id=(sh, to),
                device_id_type=MESH,
            ).start()
            return 0

        lax.fori_loop(1, ntile, send, 0, unroll=ntile <= 8)
    for s in range(planes):
        recv[s, ti] = leave[s, ti]

    for load in loads[2:]:
        load.wait()
    spot = lax.broadcasted_iota(jnp.int32, (side, side), 0)
    onehot = jnp.where(spot == order_v[...], 1.0, 0.0).astype(BF16)
    permuted = jnp.dot(onehot, rows_v[...], preferred_element_type=F32)
    filt = permuted.T.astype(BF16)

    which = lax.broadcasted_iota(jnp.int32, (count, side), 0)
    low = jnp.zeros((count, side), jnp.int32)
    for s in range(count):
        low = jnp.where(which == s, low_s[s], low)
    chi_source = (low.astype(F32) + band) / count
    for j in range(planes):
        shell = sh * planes + j
        chi_shell = (jnp.zeros((count, side), jnp.int32) + shell).astype(F32)
        chi_shell = (chi_shell + 0.5) / count
        value = 8.0 * weight_s[shell] * chi_shell * (chi_source - chi_shell) / chi_source
        value = jnp.where((low <= shell) & (shell < low + band), value, 0.0)
        table[j] = value.astype(BF16).astype(F32)

    def shell_copy(s, source, target, send_sem):
        return pltpu.make_async_remote_copy(
            src_ref=gath.at[source, s],
            dst_ref=gath.at[source, s],
            send_sem=send_sem,
            recv_sem=shell_recv.at[source, s],
            device_id=(target, ti),
            device_id_type=MESH,
        )

    def forward(s):
        for e in range(1, nx):
            source = xpeer(nx - e)
            shell_copy(s, source, sh, x_send.at[e - 1, s]).wait_recv()
            shell_copy(s, source, partner, fwd_send.at[e - 1, s]).start()

    chunk = side // 4

    def mix(source, those, first=False, last=False):
        for c in range(0, side, chunk):
            got = [gath[source, s, pl.ds(c, chunk), :].astype(F32) for s in those]
            for j in range(planes):
                total = None if first else acc[j, pl.ds(c, chunk), :]
                for s, plane in zip(those, got):
                    term = table[j, pl.ds(source * planes + s, 1), :] * plane
                    total = term if total is None else total + term
                if last:
                    half[pl.ds(c * planes + j, chunk, stride=planes), :] = total
                else:
                    acc[j, pl.ds(c, chunk), :] = total

    for s in range(planes):
        landed = recv.at[s, pl.ds(0, ntile - 1)]
        pltpu.make_async_copy(landed, landed, a2a_recv.at[s]).wait()
        plane = recv[s]
        if blk % 16:
            plane = plane.astype(F32).reshape(side, side).astype(BF16)
        gath[sh, s] = jnp.dot(filt, plane.reshape(side, side), preferred_element_type=F32).astype(BF16)
        for e in range(1, nx):
            shell_copy(s, sh, xpeer(e), x_send.at[e - 1, s]).start()
        shell_copy(s, sh, partner, near_send.at[s]).start()
        mix(sh, [s], first=s == 0)
        if s >= 2:
            forward(s - 2)

    for s in range(max(planes - 2, 0), planes):
        forward(s)
        if s < planes - 1:
            for t in range(planes):
                shell_copy(t, partner, sh, near_send.at[t]).wait_recv()
            mix(partner, list(range(planes)))
    for e in range(1, nx):
        mix(xpeer(nx - e), list(range(planes)))
    for e in range(1, nx):
        source = lax.rem(xi + nx - e, nx) * CORES + (1 - core)
        for s in range(planes):
            shell_copy(s, source, sh, fwd_send.at[e - 1, s]).wait_recv()
            mix(source, [s], last=e == nx - 1 and s == planes - 1)
    out[...] = half[...].astype(BF16).reshape(out.shape)

    gone = leave.at[pl.ds(0, planes), pl.ds(0, ntile - 1)]
    pltpu.make_async_copy(gone, gone, a2a_send).wait()
    for s in range(planes):
        shell_copy(s, sh, partner, near_send.at[s]).wait_send()
        for e in range(1, nx):
            shell_copy(s, sh, xpeer(e), x_send.at[e - 1, s]).wait_send()
            shell_copy(s, xpeer(nx - e), partner, fwd_send.at[e - 1, s]).wait_send()


def shards(residual, tile_ray, filter_rows, filter_cols, band_lo, shell_weight):
    planes, rays = residual.shape
    nshell, ntile = lax.axis_size("shell"), lax.axis_size("tile")
    side = filter_rows.shape[0]
    count = band_lo.shape[0]
    nx = nshell // CORES
    blk = side // ntile
    fold = 4 if side % 4 == 0 else 1
    major, group = side // fold, planes * fold
    arranged = residual.reshape(planes, side, side).transpose(1, 0, 2).reshape(major, group, side)
    operands = (arranged, tile_ray.reshape(1, side), filter_rows, filter_cols, band_lo, shell_weight)
    dma = pltpu.SemaphoreType.DMA
    result = pl.pallas_call(
        functools.partial(body, nshell, ntile, planes),
        out_shape=jax.ShapeDtypeStruct((major, group, side), BF16),
        in_specs=[pl.BlockSpec(memory_space=pltpu.HBM)] * 6,
        out_specs=pl.BlockSpec(memory_space=pltpu.VMEM),
        scratch_shapes=[
            pltpu.VMEM((major, group, side), BF16),
            pltpu.VMEM((planes, ntile, blk, side), BF16),
            pltpu.VMEM((planes, ntile, blk, side), BF16),
            pltpu.VMEM((nshell, planes, side, side), BF16),
            pltpu.VMEM((side * planes, side), F32),
            pltpu.VMEM((planes, side, side), F32),
            pltpu.VMEM((1, side), jnp.int32),
            pltpu.VMEM((side, side), BF16),
            pltpu.VMEM((side, side), BF16),
            pltpu.SMEM((count,), jnp.int32),
            pltpu.SMEM((count,), F32),
            pltpu.VMEM((planes, count, side), F32),
            dma((6,)),
            dma,
            dma((planes,)),
            dma((nx - 1, planes)),
            dma((planes,)),
            dma((nx - 1, planes)),
            dma((nshell, planes)),
        ],
        compiler_params=pltpu.CompilerParams(
            collective_id=0, has_side_effects=True, vmem_limit_bytes=16 * 1024 * 1024
        ),
    )(*(pltpu.with_memory_space_constraint(x, pltpu.HBM) for x in operands))
    return result.reshape(side, planes, side).transpose(1, 0, 2).reshape(planes, rays)


def solution(mesh):
    in_specs = (P("shell", "tile"), P("tile"), P(), P(), P(), P())
    out_specs = P("shell", "tile")
    return jax.shard_map(shards, mesh=mesh, in_specs=in_specs, out_specs=out_specs, check_vma=False)
```

time: 19.9 us -> 17.2 us (0.86); the launches traced: 19.5 us -> 17 us
  local copies, waits for them, and re-layouts: 3.76 us -> 0.66 us
  Pallas kernels: 15.8 us -> 16.4 us
    unnamed x13 -> x1, local copies, waits for them, and re-layouts: 3.76 us -> 0.66 us
    pallas_call x1, Pallas kernels: 15.8 us -> 16.4 us  [shards(): pl.pallas_call(functools.partial(body, nshell, ntile, planes), out_shape=...]
where the time goes in v2:
time: 17.2 us; the launch traced here: 17 us
  Pallas kernels  16.4 us (95%)
  local copies, waits for them, and re-layouts  0.66 us (4%)
    pallas_call x1, Pallas kernels, shards(): pl.pallas_call(functools.partial(body, nshell, ntile, planes), out_shape=...  16.4 us
    unnamed x1, local copies, waits for them, and re-layouts  0.66 us

profile of v2, /device:TPU:0, one launch (start us, length us, event | category | flops | bytes accessed | tf_op | source)
XLA Modules:
  0.0 17.0 jit_solution(17496013700562275062)
XLA Ops:
  0.0 16.4 %shard_map.64 = bf16[32,16,128]{2,1,0:T(8,128)(2,1)S(1)} custom-call(bf16[32,16,128]{2,1,0:T(8,128)(2,1)} %bitcast.12, s32[1,128]{1,0:T(1,128)} %bitcast.13, bf16[128,128]{1,0:T(8,128)(2,1)} %rows_in.1, bf16[128,128]{1,0:T(8,128)(2,1)} %cols_in.1, s32[16]{0:T(128)} %low_in.1, f32[16]{0:T(128)} %weight_in.1), custom_call_target="tpu_custom_call" | custom-call | tf_op jit(solution)/shard_map/pallas_call | solution.py:183
  16.4 0.7 %copy.10 = bf16[4,16384]{1,0:T(4,128)(2,1)} copy(bf16[4,16384]{1,0:T(4,128)(2,1)S(1)} %bitcast.11) | data formatting | bytes 262144

commit v3 on v2

--- a/solution.py
+++ b/solution.py
@@ -9,6 +9,7 @@
 
 MESH = pl.DeviceIdType.MESH
 CORES = 2
+PARTS = 2
 F32 = jnp.float32
 BF16 = jnp.bfloat16
 
@@ -56,28 +57,29 @@
     if mine.shape[1] % 16:
         mine = mine.astype(F32).reshape(half.shape).astype(BF16)
     half[...] = jnp.dot(mine.reshape(half.shape), cols_v[...], preferred_element_type=F32)
-    for s in range(planes):
-        leave[s] = half[pl.ds(s, side, stride=planes), :].reshape(ntile, blk, side).astype(BF16)
-
-    pl.semaphore_wait(barrier, ntile - 1 + nx)
-
-    for s in range(planes):
+    parts, _, per = leave.shape[:3]
+    for h in range(parts):
+        for p in range(per):
+            plane = half[pl.ds(h * per + p, side, stride=planes), :]
+            leave[h, :, p] = plane.reshape(ntile, blk, side).astype(BF16)
+        if h == 0:
+            pl.semaphore_wait(barrier, ntile - 1 + nx)
 
         def send(e, _):
             to = lax.rem(ti + e, ntile)
             pltpu.make_async_remote_copy(
-                src_ref=leave.at[s, to],
-                dst_ref=recv.at[s, ti],
+                src_ref=leave.at[h, to],
+                dst_ref=recv.at[h, ti],
                 send_sem=a2a_send,
-                recv_sem=a2a_recv.at[s],
+                recv_sem=a2a_recv.at[h],
                 device_id=(sh, to),
                 device_id_type=MESH,
             ).start()
             return 0
 
         lax.fori_loop(1, ntile, send, 0, unroll=ntile <= 8)
-    for s in range(planes):
-        recv[s, ti] = leave[s, ti]
+    for h in range(parts):
+        recv[h, ti] = leave[h, ti]
 
     for load in loads[2:]:
         load.wait()
@@ -118,7 +120,8 @@
     chunk = side // 4
 
     def mix(source, those, first=False, last=False):
-        for c in range(0, side, chunk):
+        def rows(i, _):
+            c = i * chunk if last else pl.multiple_of(i * chunk, chunk)
             got = [gath[source, s, pl.ds(c, chunk), :].astype(F32) for s in those]
             for j in range(planes):
                 total = None if first else acc[j, pl.ds(c, chunk), :]
@@ -129,11 +132,20 @@
                     half[pl.ds(c * planes + j, chunk, stride=planes), :] = total
                 else:
                     acc[j, pl.ds(c, chunk), :] = total
+            return 0
+
+        if last:
+            for i in range(side // chunk):
+                rows(i, 0)
+        else:
+            lax.fori_loop(0, side // chunk, rows, 0)
 
     for s in range(planes):
-        landed = recv.at[s, pl.ds(0, ntile - 1)]
-        pltpu.make_async_copy(landed, landed, a2a_recv.at[s]).wait()
-        plane = recv[s]
+        h, p = s // per, s % per
+        if p == 0:
+            landed = recv.at[h, pl.ds(0, ntile - 1)]
+            pltpu.make_async_copy(landed, landed, a2a_recv.at[h]).wait()
+        plane = recv[h, :, p]
         if blk % 16:
             plane = plane.astype(F32).reshape(side, side).astype(BF16)
         gath[sh, s] = jnp.dot(filt, plane.reshape(side, side), preferred_element_type=F32).astype(BF16)
@@ -159,7 +171,7 @@
             mix(source, [s], last=e == nx - 1 and s == planes - 1)
     out[...] = half[...].astype(BF16).reshape(out.shape)
 
-    gone = leave.at[pl.ds(0, planes), pl.ds(0, ntile - 1)]
+    gone = leave.at[pl.ds(0, parts), pl.ds(0, ntile - 1)]
     pltpu.make_async_copy(gone, gone, a2a_send).wait()
     for s in range(planes):
         shell_copy(s, sh, partner, near_send.at[s]).wait_send()
@@ -187,8 +199,8 @@
         out_specs=pl.BlockSpec(memory_space=pltpu.VMEM),
         scratch_shapes=[
             pltpu.VMEM((major, group, side), BF16),
-            pltpu.VMEM((planes, ntile, blk, side), BF16),
-            pltpu.VMEM((planes, ntile, blk, side), BF16),
+            pltpu.VMEM((PARTS, ntile, planes // PARTS, blk, side), BF16),
+            pltpu.VMEM((PARTS, ntile, planes // PARTS, blk, side), BF16),
             pltpu.VMEM((nshell, planes, side, side), BF16),
             pltpu.VMEM((side * planes, side), F32),
             pltpu.VMEM((planes, side, side), F32),
@@ -200,7 +212,7 @@
             pltpu.VMEM((planes, count, side), F32),
             dma((6,)),
             dma,
-            dma((planes,)),
+            dma((PARTS,)),
             dma((nx - 1, planes)),
             dma((planes,)),
             dma((nx - 1, planes)),

time: 17.2 us -> 17.2 us (level)
  no operation moved by 1% of the time
where the time goes in v3:
time: 17.2 us; the launch traced here: 17.1 us
  Pallas kernels  16.4 us (95%)
  local copies, waits for them, and re-layouts  0.66 us (4%)
    pallas_call x1, Pallas kernels, shards(): pl.pallas_call(functools.partial(body, nshell, ntile, planes), out_shape=...  16.4 us
    unnamed x1, local copies, waits for them, and re-layouts  0.66 us

profile of v3, /device:TPU:0, one launch (start us, length us, event | category | flops | bytes accessed | tf_op | source)
XLA Modules:
  0.0 17.1 jit_solution(15256640633778168247)
XLA Ops:
  0.0 16.4 %shard_map.64 = bf16[32,16,128]{2,1,0:T(8,128)(2,1)S(1)} custom-call(bf16[32,16,128]{2,1,0:T(8,128)(2,1)} %bitcast.12, s32[1,128]{1,0:T(1,128)} %bitcast.13, bf16[128,128]{1,0:T(8,128)(2,1)} %rows_in.1, bf16[128,128]{1,0:T(8,128)(2,1)} %cols_in.1, s32[16]{0:T(128)} %low_in.1, f32[16]{0:T(128)} %weight_in.1), custom_call_target="tpu_custom_call" | custom-call | tf_op jit(solution)/shard_map/pallas_call | solution.py:195
  16.4 0.7 %copy.10 = bf16[4,16384]{1,0:T(4,128)(2,1)} copy(bf16[4,16384]{1,0:T(4,128)(2,1)S(1)} %bitcast.11) | data formatting | bytes 262144

commit v4 on v3

--- a/solution.py
+++ b/solution.py
@@ -9,7 +9,6 @@
 
 MESH = pl.DeviceIdType.MESH
 CORES = 2
-PARTS = 2
 F32 = jnp.float32
 BF16 = jnp.bfloat16
 
@@ -18,13 +17,12 @@
     nshell, ntile, planes,
     rays, order, rows_in, cols_in, low_in, weight_in,
     out,
-    stage, leave, recv, gath, half, acc, order_v, rows_v, cols_v, low_s, weight_s, table,
+    stage, gath, half, acc, order_v, rows_v, cols_v, low_s, weight_s, table,
     local_sem, a2a_send, a2a_recv, x_send, near_send, fwd_send, shell_recv,
 ):
     side = rows_v.shape[0]
     count = nshell * planes
     band = count // 2
-    blk = side // ntile
     nx = nshell // CORES
     sh, ti = lax.axis_index("shell"), lax.axis_index("tile")
     xi, core = sh // CORES, lax.rem(sh, CORES)
@@ -44,44 +42,31 @@
     for e in range(1, nx):
         pl.semaphore_signal(barrier, inc=1, device_id=(xpeer(e), ti), device_id_type=MESH)
 
+    lead = rays.shape[0] // ntile
+    own = pl.ds(ti * lead, lead)
     pairs = [
-        (rays, stage), (cols_in, cols_v), (order, order_v), (rows_in, rows_v), (low_in, low_s), (weight_in, weight_s)
+        (rays.at[own], stage.at[own]), (order, order_v), (rows_in, rows_v), (cols_in, cols_v), (low_in, low_s), (weight_in, weight_s)
     ]
     loads = [pltpu.make_async_copy(src, dst, local_sem.at[i]) for i, (src, dst) in enumerate(pairs)]
     for load in loads:
         load.start()
-
-    loads[0].wait()
-    loads[1].wait()
-    mine = stage[...]
-    if mine.shape[1] % 16:
-        mine = mine.astype(F32).reshape(half.shape).astype(BF16)
-    half[...] = jnp.dot(mine.reshape(half.shape), cols_v[...], preferred_element_type=F32)
-    parts, _, per = leave.shape[:3]
-    for h in range(parts):
-        for p in range(per):
-            plane = half[pl.ds(h * per + p, side, stride=planes), :]
-            leave[h, :, p] = plane.reshape(ntile, blk, side).astype(BF16)
-        if h == 0:
-            pl.semaphore_wait(barrier, ntile - 1 + nx)
-
-        def send(e, _):
-            to = lax.rem(ti + e, ntile)
-            pltpu.make_async_remote_copy(
-                src_ref=leave.at[h, to],
-                dst_ref=recv.at[h, ti],
-                send_sem=a2a_send,
-                recv_sem=a2a_recv.at[h],
-                device_id=(sh, to),
-                device_id_type=MESH,
-            ).start()
-            return 0
-
-        lax.fori_loop(1, ntile, send, 0, unroll=ntile <= 8)
-    for h in range(parts):
-        recv[h, ti] = leave[h, ti]
-
-    for load in loads[2:]:
+    pl.semaphore_wait(barrier, ntile - 1 + nx)
+
+    def send(e, _):
+        to = lax.rem(ti + e, ntile)
+        pltpu.make_async_remote_copy(
+            src_ref=rays.at[pl.ds(to * lead, lead)],
+            dst_ref=stage.at[own],
+            send_sem=a2a_send,
+            recv_sem=a2a_recv,
+            device_id=(sh, to),
+            device_id_type=MESH,
+        ).start()
+        return 0
+
+    lax.fori_loop(1, ntile, send, 0, unroll=ntile <= 8)
+
+    for load in loads:
         load.wait()
     spot = lax.broadcasted_iota(jnp.int32, (side, side), 0)
     onehot = jnp.where(spot == order_v[...], 1.0, 0.0).astype(BF16)
@@ -140,25 +125,22 @@
         else:
             lax.fori_loop(0, side // chunk, rows, 0)
 
+    landed = stage.at[pl.ds(0, (ntile - 1) * lead)]
+    pltpu.make_async_copy(landed, landed, a2a_recv).wait()
+    pixels = stage[...]
+    if pixels.shape[1] % 16:
+        pixels = pixels.astype(F32).reshape(half.shape).astype(BF16)
+    half[...] = jnp.dot(pixels.reshape(half.shape), cols_v[...], preferred_element_type=F32)
     for s in range(planes):
-        h, p = s // per, s % per
-        if p == 0:
-            landed = recv.at[h, pl.ds(0, ntile - 1)]
-            pltpu.make_async_copy(landed, landed, a2a_recv.at[h]).wait()
-        plane = recv[h, :, p]
-        if blk % 16:
-            plane = plane.astype(F32).reshape(side, side).astype(BF16)
-        gath[sh, s] = jnp.dot(filt, plane.reshape(side, side), preferred_element_type=F32).astype(BF16)
+        plane = half[pl.ds(s, side, stride=planes), :].astype(BF16)
+        gath[sh, s] = jnp.dot(filt, plane, preferred_element_type=F32).astype(BF16)
         for e in range(1, nx):
             shell_copy(s, sh, xpeer(e), x_send.at[e - 1, s]).start()
         shell_copy(s, sh, partner, near_send.at[s]).start()
-        mix(sh, [s], first=s == 0)
-        if s >= 2:
-            forward(s - 2)
-
-    for s in range(max(planes - 2, 0), planes):
+    mix(sh, list(range(planes)), first=True)
+    for s in range(planes):
         forward(s)
-        if s < planes - 1:
+        if s == 0:
             for t in range(planes):
                 shell_copy(t, partner, sh, near_send.at[t]).wait_recv()
             mix(partner, list(range(planes)))
@@ -171,7 +153,7 @@
             mix(source, [s], last=e == nx - 1 and s == planes - 1)
     out[...] = half[...].astype(BF16).reshape(out.shape)
 
-    gone = leave.at[pl.ds(0, parts), pl.ds(0, ntile - 1)]
+    gone = rays.at[pl.ds(0, (ntile - 1) * lead)]
     pltpu.make_async_copy(gone, gone, a2a_send).wait()
     for s in range(planes):
         shell_copy(s, sh, partner, near_send.at[s]).wait_send()
@@ -187,7 +169,7 @@
     count = band_lo.shape[0]
     nx = nshell // CORES
     blk = side // ntile
-    fold = 4 if side % 4 == 0 else 1
+    fold = 4 if blk % 4 == 0 else 1
     major, group = side // fold, planes * fold
     arranged = residual.reshape(planes, side, side).transpose(1, 0, 2).reshape(major, group, side)
     operands = (arranged, tile_ray.reshape(1, side), filter_rows, filter_cols, band_lo, shell_weight)
@@ -199,8 +181,6 @@
         out_specs=pl.BlockSpec(memory_space=pltpu.VMEM),
         scratch_shapes=[
             pltpu.VMEM((major, group, side), BF16),
-            pltpu.VMEM((PARTS, ntile, planes // PARTS, blk, side), BF16),
-            pltpu.VMEM((PARTS, ntile, planes // PARTS, blk, side), BF16),
             pltpu.VMEM((nshell, planes, side, side), BF16),
             pltpu.VMEM((side * planes, side), F32),
             pltpu.VMEM((planes, side, side), F32),
@@ -212,7 +192,7 @@
             pltpu.VMEM((planes, count, side), F32),
             dma((6,)),
             dma,
-            dma((PARTS,)),
+            dma,
             dma((nx - 1, planes)),
             dma((planes,)),
             dma((nx - 1, planes)),

time: 17.2 us -> 16.2 us (0.942)
  Pallas kernels: 16.4 us -> 15.4 us
    pallas_call x1, Pallas kernels: 16.4 us -> 15.4 us  [shards(): pl.pallas_call(functools.partial(body, nshell, ntile, planes), out_shape=...]
where the time goes in v4:
time: 16.2 us; the launch traced here: 16.1 us
  Pallas kernels  15.4 us (95%)
  local copies, waits for them, and re-layouts  0.66 us (4%)
    pallas_call x1, Pallas kernels, shards(): pl.pallas_call(functools.partial(body, nshell, ntile, planes), out_shape=...  15.4 us
    unnamed x1, local copies, waits for them, and re-layouts  0.66 us

profile of v4, /device:TPU:0, one launch (start us, length us, event | category | flops | bytes accessed | tf_op | source)
XLA Modules:
  0.0 16.1 jit_solution(16503743975170396855)
XLA Ops:
  0.0 15.4 %shard_map.64 = bf16[32,16,128]{2,1,0:T(8,128)(2,1)S(1)} custom-call(bf16[32,16,128]{2,1,0:T(8,128)(2,1)} %bitcast.12, s32[1,128]{1,0:T(1,128)} %bitcast.13, bf16[128,128]{1,0:T(8,128)(2,1)} %rows_in.1, bf16[128,128]{1,0:T(8,128)(2,1)} %cols_in.1, s32[16]{0:T(128)} %low_in.1, f32[16]{0:T(128)} %weight_in.1), custom_call_target="tpu_custom_call" | custom-call | tf_op jit(solution)/shard_map/pallas_call | solution.py:177
  15.4 0.7 %copy.10 = bf16[4,16384]{1,0:T(4,128)(2,1)} copy(bf16[4,16384]{1,0:T(4,128)(2,1)S(1)} %bitcast.11) | data formatting | bytes 262144

commit v5 on v4

--- a/solution.py
+++ b/solution.py
@@ -102,6 +102,12 @@
             shell_copy(s, source, sh, x_send.at[e - 1, s]).wait_recv()
             shell_copy(s, source, partner, fwd_send.at[e - 1, s]).start()
 
+    def over_x(s, start):
+        for e in range(1, nx):
+            copy = shell_copy(s, sh, xpeer(e), x_send.at[e - 1, s])
+            copy.start() if start else copy.wait_send()
+
+    ahead = planes // 2
     chunk = side // 4
 
     def mix(source, those, first=False, last=False):
@@ -134,31 +140,37 @@
     for s in range(planes):
         plane = half[pl.ds(s, side, stride=planes), :].astype(BF16)
         gath[sh, s] = jnp.dot(filt, plane, preferred_element_type=F32).astype(BF16)
-        for e in range(1, nx):
-            shell_copy(s, sh, xpeer(e), x_send.at[e - 1, s]).start()
+        if s < ahead:
+            over_x(s, True)
         shell_copy(s, sh, partner, near_send.at[s]).start()
-    mix(sh, list(range(planes)), first=True)
+    for s in range(ahead, planes):
+        over_x(s - ahead, False)
+        over_x(s, True)
+        if s == ahead:
+            mix(sh, list(range(planes)), first=True)
+    for s in range(planes):
+        shell_copy(s, partner, sh, near_send.at[s]).wait_recv()
+    mix(partner, list(range(planes)))
     for s in range(planes):
         forward(s)
-        if s == 0:
-            for t in range(planes):
-                shell_copy(t, partner, sh, near_send.at[t]).wait_recv()
-            mix(partner, list(range(planes)))
     for e in range(1, nx):
         mix(xpeer(nx - e), list(range(planes)))
     for e in range(1, nx):
         source = lax.rem(xi + nx - e, nx) * CORES + (1 - core)
-        for s in range(planes):
-            shell_copy(s, source, sh, fwd_send.at[e - 1, s]).wait_recv()
-            mix(source, [s], last=e == nx - 1 and s == planes - 1)
+        for s in range(0, planes, ahead):
+            those = list(range(s, s + ahead))
+            for t in those:
+                shell_copy(t, source, sh, fwd_send.at[e - 1, t]).wait_recv()
+            mix(source, those, last=e == nx - 1 and s == planes - ahead)
     out[...] = half[...].astype(BF16).reshape(out.shape)
 
     gone = rays.at[pl.ds(0, (ntile - 1) * lead)]
     pltpu.make_async_copy(gone, gone, a2a_send).wait()
     for s in range(planes):
         shell_copy(s, sh, partner, near_send.at[s]).wait_send()
+        if s >= planes - ahead:
+            over_x(s, False)
         for e in range(1, nx):
-            shell_copy(s, sh, xpeer(e), x_send.at[e - 1, s]).wait_send()
             shell_copy(s, xpeer(nx - e), partner, fwd_send.at[e - 1, s]).wait_send()
 
 

time: 16.2 us -> 17.1 us (1.056)
  Pallas kernels: 15.4 us -> 16.3 us
    pallas_call x1, Pallas kernels: 15.4 us -> 16.3 us  [shards(): pl.pallas_call(functools.partial(body, nshell, ntile, planes), out_shape=...]
where the time goes in v5:
time: 17.1 us; the launch traced here: 17 us
  Pallas kernels  16.3 us (95%)
  local copies, waits for them, and re-layouts  0.66 us (4%)
    pallas_call x1, Pallas kernels, shards(): pl.pallas_call(functools.partial(body, nshell, ntile, planes), out_shape=...  16.3 us
    unnamed x1, local copies, waits for them, and re-layouts  0.66 us

profile of v5, /device:TPU:0, one launch (start us, length us, event | category | flops | bytes accessed | tf_op | source)
XLA Modules:
  0.0 17.0 jit_solution(6919141381533851498)
XLA Ops:
  0.0 16.3 %shard_map.64 = bf16[32,16,128]{2,1,0:T(8,128)(2,1)S(1)} custom-call(bf16[32,16,128]{2,1,0:T(8,128)(2,1)} %bitcast.12, s32[1,128]{1,0:T(1,128)} %bitcast.13, bf16[128,128]{1,0:T(8,128)(2,1)} %rows_in.1, bf16[128,128]{1,0:T(8,128)(2,1)} %cols_in.1, s32[16]{0:T(128)} %low_in.1, f32[16]{0:T(128)} %weight_in.1), custom_call_target="tpu_custom_call" | custom-call | tf_op jit(solution)/shard_map/pallas_call | solution.py:189
  16.3 0.7 %copy.10 = bf16[4,16384]{1,0:T(4,128)(2,1)} copy(bf16[4,16384]{1,0:T(4,128)(2,1)S(1)} %bitcast.11) | data formatting | bytes 262144
